TPU v7x, 512 devices: a whole 4x4x16 slice. The times are simulated.
512 devices in a mesh: sect: 2 (over y_hi), exp: 32 (over z, y_lo), dp: 8 (over x, core).
Axes of the slice: x: 4, y: 4 (y_hi: 2, y_lo: 2; y = y_hi * 2 + y_lo), z: 16, core: 2. Of those that a mesh axis runs over, the one named last changes fastest.
Arguments:
- decode_states: bfloat16 [1024, 2048], P('exp'), may hold values from -15 to 15
- norm_gain: float32 [2048], replicated, may hold values from 0.25 to 1.75
- decode_routes: int32 [4, 1024, 2], P(None, 'exp'), may hold values from 0 to 31, all different within a row; in each aligned block of 32 rows (0 to 31, 32 to 63, ..., all dimensions but the last counted through in order) at most 3 rows name the same one
- decode_gates: float32 [4, 1024, 2], P(None, 'exp'), may hold values from 0.2 to 1
- up_weight: bfloat16 [2, 32, 1536, 2048], P('sect', 'exp', 'dp'), may hold values from -5 to 5
- down_weight: bfloat16 [2, 32, 1536, 2048], P('sect', 'exp', 'dp'), may hold values from -5 to 5
- traj_inputs: bfloat16 [2, 1024, 2048], P('sect', 'exp'), may hold values from -6 to 6
- traj_cotangents: bfloat16 [2, 1024, 2048], P('sect', 'exp'), may hold values from -6 to 6
- traj_lengths: int32 [32, 2, 16], P('exp'), may hold values from 1 to 4, 32 in all within a row
- packing: int32 [32, 32], P('exp'), may hold values from 0 to 31, each once within a row
- learner_routes: int32 [4096, 2], P('exp'), may hold values from 0 to 31, all different within a row; in each aligned block of 128 rows (0 to 127, 128 to 255, ...) at most 12 rows name the same one
- learner_gates: float32 [4096, 2], P('exp'), may hold values from 0.2 to 1
Outputs:
- final_states: bfloat16 [1024, 2048], P('exp', 'sect')
- fresh_up: bfloat16 [2, 32, 1536, 2048], P('sect', 'exp', 'dp')
- fresh_down: bfloat16 [2, 32, 1536, 2048], P('sect', 'exp', 'dp')
Inputs may be any that keep to these rules, and one draw needn't show every extreme that they name: `decode_routes`: within each aligned block of 32 rows of one step (the rows of one index of exp), no expert is named more than 3 times, and that bound is met. `learner_routes`: within each aligned block of 128 rows (the slots of one learner shard), no expert is named more than 12 times, and that bound is met. `traj_lengths`: each row of 16 lengths sums to 32 and its largest is 4. `packing`: each row is a permutation of the 32 learner shards, so every holder sends exactly one trajectory to every shard.
All inputs are finite; a program needn't handle non-finite values.
Results may differ from a plain program's by a relative error of at most 0.02.
Values may be sent and summed in bfloat16 or wider, within the bound.
A program may use at most 64 MiB of HBM per device.

v0:
```python
import jax
import jax.numpy as jnp
from jax import lax
from jax.sharding import PartitionSpec as P

step_size = 3.0
norm_eps = 1e-06


def partner(array, axis, apart):
    return lax.ppermute(array, axis, [(i, i ^ 1 << apart) for i in range(lax.axis_size(axis))])


def slot_table(routes, experts, capacity):
    flat_routes = routes.reshape(-1)
    member = (flat_routes[:, None] == jnp.arange(experts, dtype=jnp.int32)[None, :]).astype(
        jnp.int32
    )
    earlier = jnp.cumsum(member, axis=0) - member
    within = jnp.sum(earlier * member, axis=1)
    target = flat_routes * capacity + within
    one_hot = (target[:, None] == jnp.arange(experts * capacity, dtype=jnp.int32)[None, :]).astype(
        jnp.float32
    )
    return one_hot.reshape(routes.shape[0], routes.shape[1], experts * capacity)


def pack_trajectories(held_rows, lengths, row_pack, capacity):
    traj_count = lengths.shape[1]
    per_half = held_rows.shape[0] // 2
    column_ids = jnp.arange(row_pack.shape[0], dtype=jnp.int32)
    starts = jnp.cumsum(lengths, axis=1) - lengths
    matches = (row_pack[None, :] == column_ids[:, None]).astype(jnp.int32)
    chosen = jnp.sum(matches * column_ids[None, :], axis=1)
    half_index = chosen // traj_count
    length_of = jnp.take(lengths.reshape(-1), chosen)
    first_row = half_index * per_half + jnp.take(starts.reshape(-1), chosen)
    offsets = jnp.arange(capacity, dtype=jnp.int32)
    in_length = offsets[None, :] < length_of[:, None]
    row_index = jnp.where(in_length, first_row[:, None] + offsets[None, :], 0).reshape(-1)
    picked = jnp.take(held_rows, row_index, axis=0)
    return jnp.where(in_length.reshape(-1)[:, None, None], picked, jnp.zeros_like(picked))


def across(block):
    return partner(block, "sect", 0)


def to_experts(payload):
    arrived = lax.all_to_all(payload, "exp", split_axis=0, concat_axis=0, tiled=True)
    return arrived


def sum_and_return(partial_out):
    summed = lax.psum(partial_out.astype(jnp.bfloat16), "dp")
    returned = lax.all_to_all(summed, "exp", split_axis=0, concat_axis=0, tiled=True)
    return returned


def expert_forward(arrived, up_slice, down_slice, hidden_total):
    inputs = arrived[:, 0, :]
    before_act = jnp.einsum(
        "sd,hd->sh", inputs, up_slice, preferred_element_type=jnp.float32
    ) * inputs.shape[1] ** (-0.5)
    activated = jax.nn.silu(before_act).astype(jnp.bfloat16)
    return jnp.einsum(
        "sh,hd->sd", activated, down_slice, preferred_element_type=jnp.float32
    ) * hidden_total ** (-0.5)


def learner_update(arrived, up_slice, down_slice, hidden_total):
    inputs = arrived[:, 0, :]
    scaled_grad = arrived[:, 1, :]
    model_scale = inputs.shape[1] ** (-0.5)
    hidden_scale = hidden_total ** (-0.5)
    before_act = (
        jnp.einsum("sd,hd->sh", inputs, up_slice, preferred_element_type=jnp.float32) * model_scale
    )
    sigmoid_val = jax.nn.sigmoid(before_act)
    activated = (before_act * sigmoid_val).astype(jnp.bfloat16)
    hidden_grad = (
        jnp.einsum("sd,hd->sh", scaled_grad, down_slice, preferred_element_type=jnp.float32)
        * hidden_scale
    )
    pre_grad = (hidden_grad * sigmoid_val * (1.0 + before_act * (1.0 - sigmoid_val))).astype(
        jnp.bfloat16
    )
    down_grad = (
        jnp.einsum("sh,sd->hd", activated, scaled_grad, preferred_element_type=jnp.float32)
        * hidden_scale
    )
    up_grad = (
        jnp.einsum("sh,sd->hd", pre_grad, inputs, preferred_element_type=jnp.float32) * model_scale
    )
    new_up = (up_slice.astype(jnp.float32) - step_size * up_grad).astype(jnp.bfloat16)
    new_down = (down_slice.astype(jnp.float32) - step_size * down_grad).astype(jnp.bfloat16)
    return jnp.stack([new_up, new_down])


def decode_step(
    states, norm_gain, routes, gate_values, up_slice, down_slice, is_rollout, hidden_total
):
    experts = lax.axis_size("exp")
    capacity = 3 * routes.shape[0] * routes.shape[1] // (2 * experts)
    normed = (
        states * lax.rsqrt(jnp.mean(states * states, axis=1, keepdims=True) + norm_eps) * norm_gain
    )
    normed = normed.astype(jnp.bfloat16)
    one_hot = slot_table(routes, experts, capacity)
    outgoing = jnp.einsum(
        "rks,rd->sd", one_hot.astype(jnp.bfloat16), normed, preferred_element_type=jnp.float32
    )
    arrived = to_experts(outgoing.astype(jnp.bfloat16)[:, None, :])
    partial_out = lax.cond(
        is_rollout,
        lambda: expert_forward(arrived, up_slice, down_slice, hidden_total),
        lambda: jnp.zeros((arrived.shape[0], arrived.shape[2]), jnp.float32),
    )
    returned = sum_and_return(partial_out)
    weighted = one_hot * gate_values[:, :, None]
    mixed = jnp.einsum(
        "rks,sd->rd", weighted, returned.astype(jnp.float32), precision=lax.Precision.HIGHEST
    )
    return states + mixed


def on_device(
    decode_states,
    norm_gain,
    decode_routes,
    decode_gates,
    up_weight,
    down_weight,
    traj_inputs,
    traj_cotangents,
    traj_lengths,
    packing,
    learner_routes,
    learner_gates,
):
    experts = lax.axis_size("exp")
    is_learner = lax.axis_index("sect") == 1
    is_rollout = jnp.logical_not(is_learner)
    up_here = up_weight[0, 0]
    down_here = down_weight[0, 0]
    hidden_total = up_here.shape[0] * lax.axis_size("dp")
    held_pair = jnp.stack([traj_inputs[0], traj_cotangents[0]], axis=1)
    crossed = across(held_pair)
    held_rows = jnp.concatenate([crossed, held_pair], axis=0)

    def run_steps(states, first_step, last_step, up_mat, down_mat):
        for step_index in range(first_step, last_step):
            states = decode_step(
                states,
                norm_gain,
                decode_routes[step_index],
                decode_gates[step_index],
                up_mat,
                down_mat,
                is_rollout,
                hidden_total,
            )
        return states

    total_steps = decode_routes.shape[0]
    half_steps = total_steps // 2
    states = decode_states.astype(jnp.float32)
    capacity_t = learner_routes.shape[0] // experts
    outgoing = pack_trajectories(held_rows, traj_lengths[0], packing[0], capacity_t)
    packed = lax.all_to_all(outgoing, "exp", split_axis=0, concat_axis=0, tiled=True)
    capacity_l = 3 * learner_routes.shape[0] * learner_routes.shape[1] // (2 * experts)
    one_hot = slot_table(learner_routes, experts, capacity_l).astype(jnp.bfloat16)
    token_part = jnp.einsum(
        "rks,rd->sd", one_hot, packed[:, 0, :], preferred_element_type=jnp.float32
    )
    scaled_rows = (learner_gates[:, :, None] * packed[:, 1, None, :].astype(jnp.float32)).astype(
        jnp.bfloat16
    )
    grad_part = jnp.einsum("rks,rkd->sd", one_hot, scaled_rows, preferred_element_type=jnp.float32)
    payload = jnp.stack([token_part, grad_part], axis=1).astype(jnp.bfloat16)
    arrived = to_experts(payload)
    fresh_pair = lax.cond(
        is_learner,
        lambda: learner_update(arrived, up_here, down_here, hidden_total),
        lambda: jnp.zeros((2,) + up_here.shape, jnp.bfloat16),
    )
    returned = across(fresh_pair)
    fresh_here = jnp.where(is_learner, fresh_pair, returned)
    states = run_steps(states, 0, half_steps, up_here, down_here)
    states = run_steps(states, half_steps, total_steps, fresh_here[0], fresh_here[1])
    half_width = states.shape[1] // 2
    own_half = states[:, :half_width].astype(jnp.bfloat16)
    other_half = states[:, half_width:].astype(jnp.bfloat16)
    delivered = across(other_half)
    final_states = jnp.where(is_learner, delivered, own_half)
    return (final_states, fresh_here[0][None, None], fresh_here[1][None, None])


def solution(mesh):
    in_specs = (
        P("exp", None),
        P(),
        P(None, "exp", None),
        P(None, "exp", None),
        P("sect", "exp", "dp", None),
        P("sect", "exp", "dp", None),
        P("sect", "exp", None),
        P("sect", "exp", None),
        P("exp", None, None),
        P("exp", None),
        P("exp", None),
        P("exp", None),
    )
    out_specs = (P("exp", "sect"), P("sect", "exp", "dp", None), P("sect", "exp", "dp", None))
    return jax.shard_map(
        on_device, mesh=mesh, in_specs=in_specs, out_specs=out_specs, check_vma=False
    )
```

profile of v0, /device:TPU:14, one launch (start us, length us, event | category | flops | bytes accessed | tf_op | source)
XLA Modules:
  0.0 829.9 jit_solution(11071036561187698457)
XLA Ops:
  7.2 0.7 fusion.96
  10.9 0.7 slice_bitcast_fusion.22
  11.7 1.0 fusion.73
  12.7 0.7 bitcast_add_fusion
  13.5 1.2 fusion.64
  15.3 0.9 reduce.2
  16.2 1.0 reshape.297
  17.2 16.7 %all-to-all-start = ((bf16[32,2,3072]{2,1,0:T(2,128)(2,1)}), bf16[32,2,3072]{2,1,0:T(2,128)(2,1)S(1)}, u32[]{:S(2)}, u32[]{:S(2)}) async-start(bf16[32,2,3072]{2,1,0:T(2,128)(2,1)} %reshape.297), calls=%async_computation | async-start | bytes 786432 | tf_op jit(solution)/shard_map/all_to_all | solution.py:50
  34.0 27.1 %all-to-all-done = bf16[32,2,3072]{2,1,0:T(2,128)(2,1)S(1)} async-done(((bf16[32,2,3072]{2,1,0:T(2,128)(2,1)}), bf16[32,2,3072]{2,1,0:T(2,128)(2,1)S(1)}, u32[]{:S(2)}, u32[]{:S(2)}) %all-to-all-start) | async-done | bytes 393248 | tf_op jit(solution)/shard_map/all_to_all | solution.py:50
  61.4 0.8 conditional.5
  61.4 0.8 convolution_multiply_fusion
  62.2 1.0 all_to_all.51
  63.3 65.0 %all-reduce.5.cloned.1.call-done = bf16[32,3,2048]{2,1,0:T(4,128)(2,1)} async-done(((bf16[32,3,2048]{2,1,0:T(4,128)(2,1)}), bf16[32,3,2048]{2,1,0:T(4,128)(2,1)}) %all-reduce.5.cloned.1.call-update) | async-done | bytes 393232 | tf_op jit(solution)/shard_map/psum | solution.py:55
  128.3 13.8 %all-to-all-start.1 = ((bf16[32,3,2048]{2,1,0:T(4,128)(2,1)}), bf16[32,3,2048]{2,1,0:T(4,128)(2,1)S(1)}, u32[]{:S(2)}, u32[]{:S(2)}) async-start(bf16[32,3,2048]{2,1,0:T(4,128)(2,1)} %all-reduce.5.cloned.1.call-done), calls=%async_computation.1 | async-start | bytes 1048576 | tf_op jit(solution)/shard_map/all_to_all | solution.py:56
  143.2 4.0 collective-permute-start
  149.4 26.4 %all-to-all-done.1 = bf16[32,3,2048]{2,1,0:T(4,128)(2,1)S(1)} async-done(((bf16[32,3,2048]{2,1,0:T(4,128)(2,1)}), bf16[32,3,2048]{2,1,0:T(4,128)(2,1)S(1)}, u32[]{:S(2)}, u32[]{:S(2)}) %all-to-all-start.1) | async-done | bytes 393248 | tf_op jit(solution)/shard_map/all_to_all | solution.py:56
  177.6 0.9 reduce.3
  178.4 1.0 reshape.299
  179.5 4.0 all-to-all-start.2
  183.8 0.8 maximum_maximum_fusion
  184.6 2.7 gather_fusion
  187.3 2.6 broadcast_select_fusion.1
  189.8 21.4 %all-to-all-done.2 = bf16[32,2,3072]{2,1,0:T(2,128)(2,1)S(1)} async-done(((bf16[32,2,3072]{2,1,0:T(2,128)(2,1)}), bf16[32,2,3072]{2,1,0:T(2,128)(2,1)S(1)}, u32[]{:S(2)}, u32[]{:S(2)}) %all-to-all-start.2) | async-done | bytes 393248 | tf_op jit(solution)/shard_map/all_to_all | solution.py:50
  211.2 4.3 all-to-all-start.5
  216.1 2.2 conditional.6
  216.2 2.2 convolution_multiply_fusion.2
  218.3 1.0 all_to_all.55
  220.4 48.1 %all-to-all-done.5 = bf16[128,2,2048]{2,1,0:T(2,128)(2,1)S(1)} async-done(((bf16[128,2,2048]{2,1,0:T(2,128)(2,1)}), bf16[128,2,2048]{2,1,0:T(2,128)(2,1)S(1)}, u32[]{:S(2)}, u32[]{:S(2)}) %all-to-all-start.5) | async-done | bytes 1048608 | tf_op jit(solution)/shard_map/all_to_all | solution.py:170
  268.5 25.5 %all-reduce.7.cloned.1.call-done = bf16[32,3,2048]{2,1,0:T(4,128)(2,1)} async-done(((bf16[32,3,2048]{2,1,0:T(4,128)(2,1)}), bf16[32,3,2048]{2,1,0:T(4,128)(2,1)}) %all-reduce.7.cloned.1.call-update) | async-done | bytes 393232 | tf_op jit(solution)/shard_map/psum | solution.py:55
  294.0 13.8 %all-to-all-start.3 = ((bf16[32,3,2048]{2,1,0:T(4,128)(2,1)}), bf16[32,3,2048]{2,1,0:T(4,128)(2,1)S(1)}, u32[]{:S(2)}, u32[]{:S(2)}) async-start(bf16[32,3,2048]{2,1,0:T(4,128)(2,1)} %all-reduce.7.cloned.1.call-done), calls=%async_computation.3 | async-start | bytes 1048576 | tf_op jit(solution)/shard_map/all_to_all | solution.py:56
  308.2 1.5 fusion.95
  311.7 4.9 copy.159
  316.6 24.9 %all-to-all-done.3 = bf16[32,3,2048]{2,1,0:T(4,128)(2,1)S(1)} async-done(((bf16[32,3,2048]{2,1,0:T(4,128)(2,1)}), bf16[32,3,2048]{2,1,0:T(4,128)(2,1)S(1)}, u32[]{:S(2)}, u32[]{:S(2)}) %all-to-all-start.3) | async-done | bytes 393248 | tf_op jit(solution)/shard_map/all_to_all | solution.py:56
  341.5 0.8 copy-done.3
  342.3 4.1 all-to-all-start.6
  346.5 2.0 all_to_all.57
  348.6 1.5 multiply_reduce_fusion.1
  350.0 142.2 %all-to-all-done.6 = bf16[384,2,2048]{2,1,0:T(2,128)(2,1)S(1)} async-done(((bf16[384,2,2048]{2,1,0:T(2,128)(2,1)}), bf16[384,2,2048]{2,1,0:T(2,128)(2,1)S(1)}, u32[]{:S(2)}, u32[]{:S(2)}) %all-to-all-start.6) | async-done | bytes 3145760 | tf_op jit(solution)/shard_map/all_to_all | solution.py:50
  492.6 13.6 %collective-permute-start.1 = (bf16[2,192,2048]{2,1,0:T(8,128)(2,1)S(1)}, bf16[2,192,2048]{2,1,0:T(8,128)(2,1)S(1)}, u32[]{:S(2)}, u32[]{:S(2)}) collective-permute-start(bf16[2,192,2048]{2,1,0:T(8,128)(2,1)S(1)} %get-tuple-element.162), channel_id=1, source_target_pairs={{0,256},{256,0},{1,257},{257,1},{2,258},{258,2},{3,259},{259,3},{4... | collective-permute-start | bytes 4718600 | tf_op jit(solution)/shard_map/ppermute | solution.py:11
  506.2 1.1 fusion.66
  507.3 2.5 reduce.4
  509.8 2.0 reshape.301
  511.8 4.4 all-to-all-start.4
  516.3 25.9 %all-to-all-done.4 = bf16[32,2,3072]{2,1,0:T(2,128)(2,1)} async-done(((bf16[32,2,3072]{2,1,0:T(2,128)(2,1)}), bf16[32,2,3072]{2,1,0:T(2,128)(2,1)}, u32[]{:S(2)}, u32[]{:S(2)}) %all-to-all-start.4) | async-done | bytes 393248 | tf_op jit(solution)/shard_map/all_to_all | solution.py:50
  542.1 3.4 reshape.302
  545.7 1.5 slice_bitcast_fusion.18
  547.3 1.9 conditional.8
  547.3 1.9 convolution_multiply_fusion.6
  549.2 1.0 all_to_all.61
  550.3 66.9 %all-reduce.9.cloned.1.call-done = bf16[32,3,2048]{2,1,0:T(4,128)(2,1)} async-done(((bf16[32,3,2048]{2,1,0:T(4,128)(2,1)}), bf16[32,3,2048]{2,1,0:T(4,128)(2,1)}) %all-reduce.9.cloned.1.call-update) | async-done | bytes 393232 | tf_op jit(solution)/shard_map/psum | solution.py:55
  617.2 13.8 %all-to-all-start.7 = ((bf16[32,3,2048]{2,1,0:T(4,128)(2,1)}), bf16[32,3,2048]{2,1,0:T(4,128)(2,1)S(1)}, u32[]{:S(2)}, u32[]{:S(2)}) async-start(bf16[32,3,2048]{2,1,0:T(4,128)(2,1)} %all-reduce.9.cloned.1.call-done), calls=%async_computation.7 | async-start | bytes 1048576 | tf_op jit(solution)/shard_map/all_to_all | solution.py:56
  631.1 33.6 %all-to-all-done.7 = bf16[32,3,2048]{2,1,0:T(4,128)(2,1)S(1)} async-done(((bf16[32,3,2048]{2,1,0:T(4,128)(2,1)}), bf16[32,3,2048]{2,1,0:T(4,128)(2,1)S(1)}, u32[]{:S(2)}, u32[]{:S(2)}) %all-to-all-start.7) | async-done | bytes 393248 | tf_op jit(solution)/shard_map/all_to_all | solution.py:56
  665.8 0.9 reduce.5
  666.7 1.0 reshape.303
  667.7 4.0 all-to-all-start.8
  671.7 27.7 %all-to-all-done.8 = bf16[32,2,3072]{2,1,0:T(2,128)(2,1)S(1)} async-done(((bf16[32,2,3072]{2,1,0:T(2,128)(2,1)}), bf16[32,2,3072]{2,1,0:T(2,128)(2,1)S(1)}, u32[]{:S(2)}, u32[]{:S(2)}) %all-to-all-start.8) | async-done | bytes 393248 | tf_op jit(solution)/shard_map/all_to_all | solution.py:50
  699.4 1.0 reshape.304
  700.4 1.9 conditional.9
  700.4 1.9 convolution_multiply_fusion.8
  702.4 1.0 all_to_all.65
  703.4 63.5 %all-reduce.11.cloned.1.call-done = bf16[32,3,2048]{2,1,0:T(4,128)(2,1)} async-done(((bf16[32,3,2048]{2,1,0:T(4,128)(2,1)}), bf16[32,3,2048]{2,1,0:T(4,128)(2,1)}) %all-reduce.11.cloned.1.call-update) | async-done | bytes 393232 | tf_op jit(solution)/shard_map/psum | solution.py:55
  767.0 47.5 %all_to_all.78 = bf16[32,3,2048]{2,1,0:T(4,128)(2,1)S(1)} all-to-all(bf16[32,3,2048]{2,1,0:T(4,128)(2,1)} %all-reduce.11.cloned.1.call-done), channel_id=1, replica_groups=mesh['sect'=2,'exp'=32,'dp'=8] {'exp'}, dimensions={0} | all-to-all | bytes 786432 | tf_op jit(solution)/shard_map/all_to_all | solution.py:56
  815.1 4.0 collective-permute-start.2
  819.1 3.6 collective-permute-done.2
  (123 shorter events, 16.5 us)
Async XLA Ops:
  16.2 45.2 %copy-start.12 = (bf16[1,1,192,2048]{3,2,1,0:T(8,128)(2,1)S(1)}, bf16[1,1,192,2048]{3,2,1,0:T(8,128)(2,1)}, u32[]{:S(2)}) copy-start(bf16[1,1,192,2048]{3,2,1,0:T(8,128)(2,1)} %param.28) | copy-start | bytes 2359300
  16.2 45.2 %copy-start.14 = (bf16[1,1,192,2048]{3,2,1,0:T(8,128)(2,1)S(1)}, bf16[1,1,192,2048]{3,2,1,0:T(8,128)(2,1)}, u32[]{:S(2)}) copy-start(bf16[1,1,192,2048]{3,2,1,0:T(8,128)(2,1)} %param.29) | copy-start | bytes 2359300
  17.2 43.8 %all-to-all-start = ((bf16[32,2,3072]{2,1,0:T(2,128)(2,1)}), bf16[32,2,3072]{2,1,0:T(2,128)(2,1)S(1)}, u32[]{:S(2)}, u32[]{:S(2)}) async-start(bf16[32,2,3072]{2,1,0:T(2,128)(2,1)} %reshape.297), calls=%async_computation | async-start | bytes 786432 | tf_op jit(solution)/shard_map/all_to_all | solution.py:50
  33.9 94.4 %all-reduce.5.cloned.1.call-start = ((), (), s32[]{:S(2)}) async-start(), calls=%async_computation.10 | async-start | bytes 1048576 | tf_op jit(solution)/shard_map/psum | solution.py:55
  62.2 79.9 %copy-start.7 = (bf16[1,32,2048]{2,1,0:T(8,128)(2,1)S(1)}, bf16[1,32,2048]{2,1,0:T(8,128)(2,1)}, u32[]{:S(2)}) copy-start(bf16[1,32,2048]{2,1,0:T(8,128)(2,1)} %param.30) | copy-start | bytes 393220
  62.2 80.1 %copy-start.8 = (bf16[1,32,2048]{2,1,0:T(8,128)(2,1)S(1)}, bf16[1,32,2048]{2,1,0:T(8,128)(2,1)}, u32[]{:S(2)}) copy-start(bf16[1,32,2048]{2,1,0:T(8,128)(2,1)} %param.31) | copy-start | bytes 393220
  63.3 83.9 %copy-start.11 = (s32[1,2,16]{2,1,0:T(2,128)S(1)}, s32[1,2,16]{2,1,0:T(2,128)}, u32[]{:S(2)}) copy-start(s32[1,2,16]{2,1,0:T(2,128)} %param.32) | copy-start | bytes 388
  63.3 84.3 %copy-start.15 = (s32[1,32]{1,0:T(1,128)S(1)}, s32[1,32]{1,0:T(1,128)}, u32[]{:S(2)}) copy-start(s32[1,32]{1,0:T(1,128)} %param.33) | copy-start | bytes 388
  128.3 47.5 %all-to-all-start.1 = ((bf16[32,3,2048]{2,1,0:T(4,128)(2,1)}), bf16[32,3,2048]{2,1,0:T(4,128)(2,1)S(1)}, u32[]{:S(2)}, u32[]{:S(2)}) async-start(bf16[32,3,2048]{2,1,0:T(4,128)(2,1)} %all-reduce.5.cloned.1.call-done), calls=%async_computation.1 | async-start | bytes 1048576 | tf_op jit(solution)/shard_map/all_to_all | solution.py:56
  142.3 33.8 %copy-start.4 = (bf16[32,2048]{1,0:T(8,128)(2,1)S(1)}, bf16[32,2048]{1,0:T(8,128)(2,1)}, u32[]{:S(2)}) copy-start(bf16[32,2048]{1,0:T(8,128)(2,1)} %param.24) | copy-start | bytes 393220
  143.2 34.1 %copy-start.6 = (f32[2048]{0:T(1024)S(1)}, f32[2048]{0:T(1024)}, u32[]{:S(2)}) copy-start(f32[2048]{0:T(1024)} %param.25) | copy-start | bytes 24580
  143.2 40.6 %collective-permute-start = (bf16[32,2,2048]{2,1,0:T(2,128)(2,1)S(1)}, bf16[32,2,2048]{2,1,0:T(2,128)(2,1)S(1)}, u32[]{:S(2)}, u32[]{:S(2)}) collective-permute-start(bf16[32,2,2048]{2,1,0:T(2,128)(2,1)S(1)} %pad_maximum_fusion.2), channel_id=1, source_target_pairs={{0,256},{256,0},{1,257},{257,1},{2,258},{258,2},{3,259},{259,3},{4... | collective-permute-start | bytes 786440 | tf_op jit(solution)/shard_map/ppermute | solution.py:11
  176.5 0.7 copy-start.2
  179.5 31.7 %all-to-all-start.2 = ((bf16[32,2,3072]{2,1,0:T(2,128)(2,1)}), bf16[32,2,3072]{2,1,0:T(2,128)(2,1)S(1)}, u32[]{:S(2)}, u32[]{:S(2)}) async-start(bf16[32,2,3072]{2,1,0:T(2,128)(2,1)} %reshape.299), calls=%async_computation.2 | async-start | bytes 786432 | tf_op jit(solution)/shard_map/all_to_all | solution.py:50
  189.8 25.7 %copy-start.9 = (s32[128,2]{0,1:T(2,128)S(1)}, s32[128,2]{0,1:T(2,128)}, u32[]{:S(2)}) copy-start(s32[128,2]{0,1:T(2,128)} %param.34) | copy-start | bytes 3076
  211.2 57.3 %all-to-all-start.5 = ((bf16[128,2,2048]{2,1,0:T(2,128)(2,1)}), bf16[128,2,2048]{2,1,0:T(2,128)(2,1)S(1)}, u32[]{:S(2)}, u32[]{:S(2)}) async-start(bf16[128,2,2048]{2,1,0:T(2,128)(2,1)} %broadcast_select_fusion.1), calls=%async_computation.5 | async-start | bytes 2097152 | tf_op jit(solution)/shard_map/all_to_all | solution.py:170
  215.5 78.5 %all-reduce.7.cloned.1.call-start = ((), (), s32[]{:S(2)}) async-start(), calls=%async_computation.11 | async-start | bytes 1048576 | tf_op jit(solution)/shard_map/psum | solution.py:55
  294.0 47.5 %all-to-all-start.3 = ((bf16[32,3,2048]{2,1,0:T(4,128)(2,1)}), bf16[32,3,2048]{2,1,0:T(4,128)(2,1)S(1)}, u32[]{:S(2)}, u32[]{:S(2)}) async-start(bf16[32,3,2048]{2,1,0:T(4,128)(2,1)} %all-reduce.7.cloned.1.call-done), calls=%async_computation.3 | async-start | bytes 1048576 | tf_op jit(solution)/shard_map/all_to_all | solution.py:56
  310.0 0.7 copy-start.10
  341.5 0.8 copy-start.3
  342.3 149.9 %all-to-all-start.6 = ((bf16[384,2,2048]{2,1,0:T(2,128)(2,1)}), bf16[384,2,2048]{2,1,0:T(2,128)(2,1)S(1)}, u32[]{:S(2)}, u32[]{:S(2)}) async-start(bf16[384,2,2048]{2,1,0:T(2,128)(2,1)} %copy.159), calls=%async_computation.6 | async-start | bytes 6291456 | tf_op jit(solution)/shard_map/all_to_all | solution.py:50
  492.6 53.0 %collective-permute-start.1 = (bf16[2,192,2048]{2,1,0:T(8,128)(2,1)S(1)}, bf16[2,192,2048]{2,1,0:T(8,128)(2,1)S(1)}, u32[]{:S(2)}, u32[]{:S(2)}) collective-permute-start(bf16[2,192,2048]{2,1,0:T(8,128)(2,1)S(1)} %get-tuple-element.162), channel_id=1, source_target_pairs={{0,256},{256,0},{1,257},{257,1},{2,258},{258,2},{3,259},{259,3},{4... | collective-permute-start | bytes 4718600 | tf_op jit(solution)/shard_map/ppermute | solution.py:11
  511.8 30.3 %all-to-all-start.4 = ((bf16[32,2,3072]{2,1,0:T(2,128)(2,1)}), bf16[32,2,3072]{2,1,0:T(2,128)(2,1)}, u32[]{:S(2)}, u32[]{:S(2)}) async-start(bf16[32,2,3072]{2,1,0:T(2,128)(2,1)} %reshape.301), calls=%async_computation.4 | async-start | bytes 786432 | tf_op jit(solution)/shard_map/all_to_all | solution.py:50
  516.2 101.0 %all-reduce.9.cloned.1.call-start = ((), (), s32[]{:S(2)}) async-start(), calls=%async_computation.12 | async-start | bytes 1048576 | tf_op jit(solution)/shard_map/psum | solution.py:55
  617.2 47.5 %all-to-all-start.7 = ((bf16[32,3,2048]{2,1,0:T(4,128)(2,1)}), bf16[32,3,2048]{2,1,0:T(4,128)(2,1)S(1)}, u32[]{:S(2)}, u32[]{:S(2)}) async-start(bf16[32,3,2048]{2,1,0:T(4,128)(2,1)} %all-reduce.9.cloned.1.call-done), calls=%async_computation.7 | async-start | bytes 1048576 | tf_op jit(solution)/shard_map/all_to_all | solution.py:56
  667.7 31.7 %all-to-all-start.8 = ((bf16[32,2,3072]{2,1,0:T(2,128)(2,1)}), bf16[32,2,3072]{2,1,0:T(2,128)(2,1)S(1)}, u32[]{:S(2)}, u32[]{:S(2)}) async-start(bf16[32,2,3072]{2,1,0:T(2,128)(2,1)} %reshape.303), calls=%async_computation.8 | async-start | bytes 786432 | tf_op jit(solution)/shard_map/all_to_all | solution.py:50
  671.7 95.3 %all-reduce.11.cloned.1.call-start = ((), (), s32[]{:S(2)}) async-start(), calls=%async_computation.13 | async-start | bytes 1048576 | tf_op jit(solution)/shard_map/psum | solution.py:55
  815.1 7.7 collective-permute-start.2
Sparse Core Ops, SparseCore 0:
  63.4 64.8 all-reduce.4
  219.5 74.4 all-reduce.6
  550.4 66.7 all-reduce.8
  703.6 63.3 all-reduce.10
where the time goes:
time: 831 us; the launch traced here: 830 us
  waiting for transfers between devices  602 us (72%)
  starting transfers between devices  101 us (12%)
  blocking collectives  47.5 us (6%)
  local copies, waits for them, and re-layouts  35.2 us (4%)
  other arithmetic  16.6 us (2%)
  between operations  14.4 us (2%)
  matrix products  13.5 us (2%)
    all_to_all x5, waiting for transfers between devices, to_experts(): lax.all_to_all(payload, 'exp', split_axis=0, concat_axis=0, tiled=True)  244 us
    psum x4, waiting for transfers between devices, sum_and_return(): summed = lax.psum(partial_out.astype(jnp.bfloat16), 'dp')  221 us
    all_to_all x3, waiting for transfers between devices, sum_and_return(): lax.all_to_all(summed, 'exp', split_axis=0, concat_axis=0, tiled=True)  84.9 us
    all_to_all x1, waiting for transfers between devices, on_device(): lax.all_to_all(outgoing, 'exp', split_axis=0, concat_axis=0, tiled=True)  48.1 us
    all_to_all x1, blocking collectives, sum_and_return(): lax.all_to_all(summed, 'exp', split_axis=0, concat_axis=0, tiled=True)  47.5 us
    all_to_all x3, starting transfers between devices, sum_and_return(): lax.all_to_all(summed, 'exp', split_axis=0, concat_axis=0, tiled=True)  41.4 us
    all_to_all x5, starting transfers between devices, to_experts(): lax.all_to_all(payload, 'exp', split_axis=0, concat_axis=0, tiled=True)  33.2 us
    ppermute x3, starting transfers between devices, partner(): lax.ppermute(array, axis, [(i, i ^ 1 << apart) for i in range(lax.axis_si...  21.6 us
  transfers between devices with their start and end apart: 16, of which 14 were waited for; matrix products, arithmetic and copies ran while one was open for 4% of the time, Pallas kernels for 0%

commit v1 on v0

--- a/solution.py
+++ b/solution.py
@@ -1,3 +1,4 @@
+import functools
 import jax
 import jax.numpy as jnp
 from jax import lax
@@ -5,6 +6,14 @@
 
 step_size = 3.0
 norm_eps = 1e-06
+
+
+def work_the_lines(mat, group_axis):
+    piece_out = jax.lax.all_gather(mat, axis_name=group_axis).sum(axis=0)
+    return piece_out
+
+
+deliver_flows = functools.partial(work_the_lines, group_axis="dp")
 
 
 def partner(array, axis, apart):
@@ -52,7 +61,7 @@
 
 
 def sum_and_return(partial_out):
-    summed = lax.psum(partial_out.astype(jnp.bfloat16), "dp")
+    summed = deliver_flows(partial_out.astype(jnp.bfloat16))
     returned = lax.all_to_all(summed, "exp", split_axis=0, concat_axis=0, tiled=True)
     return returned
 

time: 831 us -> 654 us (0.79)
  the two profiles are of different devices: /device:TPU:14 before, /device:TPU:16 now
where the time goes in v1:
time: 654 us; the launch traced here: 653 us
  waiting for transfers between devices  435 us (67%)
  starting transfers between devices  81.1 us (12%)
  blocking collectives  46.4 us (7%)
  local copies, waits for them, and re-layouts  36.6 us (6%)
  other arithmetic  25.6 us (4%)
  between operations  14.5 us (2%)
  matrix products  13.3 us (2%)
    all_to_all x5, waiting for transfers between devices, to_experts(): lax.all_to_all(payload, 'exp', split_axis=0, concat_axis=0, tiled=True)  177 us
    all_gather x4, waiting for transfers between devices, work_the_lines(): piece_out = jax.lax.all_gather(mat, axis_name=group_axis).sum(axis=0)  109 us
    all_to_all x3, waiting for transfers between devices, sum_and_return(): lax.all_to_all(summed, 'exp', split_axis=0, concat_axis=0, tiled=True)  81.2 us
    all_to_all x1, waiting for transfers between devices, on_device(): lax.all_to_all(outgoing, 'exp', split_axis=0, concat_axis=0, tiled=True)  49 us
    all_to_all x1, blocking collectives, sum_and_return(): lax.all_to_all(summed, 'exp', split_axis=0, concat_axis=0, tiled=True)  46.4 us
    all_to_all x3, starting transfers between devices, sum_and_return(): lax.all_to_all(summed, 'exp', split_axis=0, concat_axis=0, tiled=True)  34.8 us
    all_to_all x5, starting transfers between devices, to_experts(): lax.all_to_all(payload, 'exp', split_axis=0, concat_axis=0, tiled=True)  32.9 us
    ppermute x3, waiting for transfers between devices, partner(): lax.ppermute(array, axis, [(i, i ^ 1 << apart) for i in range(lax.axis_si...  19 us
  transfers between devices with their start and end apart: 16, of which 15 were waited for; matrix products, arithmetic and copies ran while one was open for 7% of the time, Pallas kernels for 0%

profile of v1, /device:TPU:16, one launch (start us, length us, event | category | flops | bytes accessed | tf_op | source)
XLA Modules:
  0.0 652.7 jit_solution(15290496039093183195)
XLA Ops:
  7.2 0.7 fusion.96
  10.9 0.7 slice_bitcast_fusion.22
  11.7 1.0 fusion.73
  12.7 0.7 bitcast_add_fusion
  13.5 1.2 fusion.64
  15.3 0.8 reduce.6
  16.1 1.0 reshape.301
  17.1 16.2 %all-to-all-start = ((bf16[32,2,3072]{2,1,0:T(2,128)(2,1)}), bf16[32,2,3072]{2,1,0:T(2,128)(2,1)S(1)}, u32[]{:S(2)}, u32[]{:S(2)}) async-start(bf16[32,2,3072]{2,1,0:T(2,128)(2,1)} %reshape.301), calls=%async_computation | async-start | bytes 786432 | tf_op jit(solution)/shard_map/all_to_all | solution.py:59
  33.4 27.4 %all-to-all-done = bf16[32,2,3072]{2,1,0:T(2,128)(2,1)S(1)} async-done(((bf16[32,2,3072]{2,1,0:T(2,128)(2,1)}), bf16[32,2,3072]{2,1,0:T(2,128)(2,1)S(1)}, u32[]{:S(2)}, u32[]{:S(2)}) %all-to-all-start) | async-done | bytes 393248 | tf_op jit(solution)/shard_map/all_to_all | solution.py:59
  63.1 4.5 collective-permute-start
  69.7 19.9 %all-gather.9.cloned.1.call-done = bf16[768,2048]{1,0:T(8,128)(2,1)} async-done(((bf16[96,2048]{1,0:T(8,128)(2,1)}), bf16[768,2048]{1,0:T(8,128)(2,1)}) %all-gather.9.cloned.1.call-update) | async-done | bytes 3145744 | tf_op jit(solution)/shard_map/all_gather | solution.py:12
  89.5 2.5 reduce_sum.234
  92.0 1.0 all_to_all.51
  93.1 13.2 %all-to-all-start.1 = ((bf16[32,3,2048]{2,1,0:T(4,128)(2,1)}), bf16[32,3,2048]{2,1,0:T(4,128)(2,1)S(1)}, u32[]{:S(2)}, u32[]{:S(2)}) async-start(bf16[32,3,2048]{2,1,0:T(4,128)(2,1)} %all_to_all.51), calls=%async_computation.1 | async-start | bytes 1048576 | tf_op jit(solution)/shard_map/all_to_all | solution.py:65
  106.6 0.8 maximum_maximum_fusion
  107.5 2.7 gather_fusion
  110.1 2.6 broadcast_select_fusion.1
  112.7 27.0 %all-to-all-done.1 = bf16[32,3,2048]{2,1,0:T(4,128)(2,1)S(1)} async-done(((bf16[32,3,2048]{2,1,0:T(4,128)(2,1)}), bf16[32,3,2048]{2,1,0:T(4,128)(2,1)S(1)}, u32[]{:S(2)}, u32[]{:S(2)}) %all-to-all-start.1) | async-done | bytes 393248 | tf_op jit(solution)/shard_map/all_to_all | solution.py:65
  139.7 4.1 all-to-all-start.5
  146.2 0.8 reduce.7
  147.0 1.0 reshape.303
  148.1 49.0 %all-to-all-done.5 = bf16[128,2,2048]{2,1,0:T(2,128)(2,1)S(1)} async-done(((bf16[128,2,2048]{2,1,0:T(2,128)(2,1)}), bf16[128,2,2048]{2,1,0:T(2,128)(2,1)S(1)}, u32[]{:S(2)}, u32[]{:S(2)}) %all-to-all-start.5) | async-done | bytes 1048608 | tf_op jit(solution)/shard_map/all_to_all | solution.py:179
  197.1 4.9 all-to-all-start.2
  202.4 1.5 fusion.95
  205.8 4.9 copy.159
  210.7 18.5 %all-to-all-done.2 = bf16[32,2,3072]{2,1,0:T(2,128)(2,1)S(1)} async-done(((bf16[32,2,3072]{2,1,0:T(2,128)(2,1)}), bf16[32,2,3072]{2,1,0:T(2,128)(2,1)S(1)}, u32[]{:S(2)}, u32[]{:S(2)}) %all-to-all-start.2) | async-done | bytes 393248 | tf_op jit(solution)/shard_map/all_to_all | solution.py:59
  229.3 0.7 copy-done.5
  230.0 4.1 all-to-all-start.6
  234.1 3.5 reshape.304
  237.6 0.8 conditional.6
  237.6 0.8 broadcast.226
  238.4 36.3 %all-gather.11.cloned.1.call-done = bf16[768,2048]{1,0:T(8,128)(2,1)} async-done(((bf16[96,2048]{1,0:T(8,128)(2,1)}), bf16[768,2048]{1,0:T(8,128)(2,1)}) %all-gather.11.cloned.1.call-update) | async-done | bytes 3145744 | tf_op jit(solution)/shard_map/all_gather | solution.py:12
  274.7 3.3 reduce_sum.240
  278.0 2.1 all_to_all.55
  280.1 93.0 %all-to-all-done.6 = bf16[384,2,2048]{2,1,0:T(2,128)(2,1)S(1)} async-done(((bf16[384,2,2048]{2,1,0:T(2,128)(2,1)}), bf16[384,2,2048]{2,1,0:T(2,128)(2,1)S(1)}, u32[]{:S(2)}, u32[]{:S(2)}) %all-to-all-start.6) | async-done | bytes 3145760 | tf_op jit(solution)/shard_map/all_to_all | solution.py:59
  373.1 8.4 %all-to-all-start.3 = ((bf16[32,3,2048]{2,1,0:T(4,128)(2,1)}), bf16[32,3,2048]{2,1,0:T(4,128)(2,1)}, u32[]{:S(2)}, u32[]{:S(2)}) async-start(bf16[32,3,2048]{2,1,0:T(4,128)(2,1)} %all_to_all.55), calls=%async_computation.3 | async-start | bytes 1048576 | tf_op jit(solution)/shard_map/all_to_all | solution.py:65
  381.5 10.2 %conditional.7 = (bf16[2,192,2048]{2,1,0:T(8,128)(2,1)S(1)}) conditional(s32[]{:T(128)} %convert_element_type.189, () %tuple.44, (bf16[192,2048]{1,0:T(8,128)(2,1)}, bf16[384,2,2048]{2,1,0:T(2,128)(2,1)S(1)}, bf16[192,2048]{1,0:T(8,128)(2,1)}) %tuple.115), branch_computations={%region_27.29_spmd, %region_28.30_spmd} | conditional | flops 1213071360 | bytes 52789368 | solution.py:191
  381.8 1.4 copy.160
  383.2 1.7 fusion.28
  384.9 4.8 fusion.25
  389.6 1.9 fusion.24
  391.7 1.9 collective-permute-start.1
  393.7 21.0 %all-to-all-done.3 = bf16[32,3,2048]{2,1,0:T(4,128)(2,1)} async-done(((bf16[32,3,2048]{2,1,0:T(4,128)(2,1)}), bf16[32,3,2048]{2,1,0:T(4,128)(2,1)}, u32[]{:S(2)}, u32[]{:S(2)}) %all-to-all-start.3) | async-done | bytes 393248 | tf_op jit(solution)/shard_map/all_to_all | solution.py:65
  414.7 1.4 all_to_all.57
  416.8 0.8 reduce.8
  417.6 1.0 reshape.305
  418.6 3.9 all-to-all-start.4
  422.6 14.1 %collective-permute-done.1 = bf16[2,192,2048]{2,1,0:T(8,128)(2,1)} collective-permute-done((bf16[2,192,2048]{2,1,0:T(8,128)(2,1)S(1)}, bf16[2,192,2048]{2,1,0:T(8,128)(2,1)}, u32[]{:S(2)}, u32[]{:S(2)}) %collective-permute-start.1) | collective-permute-done | bytes 1572896 | tf_op jit(solution)/shard_map/ppermute | solution.py:20
  436.8 1.6 slice_bitcast_fusion.18
  438.4 10.9 %all-to-all-done.4 = bf16[32,2,3072]{2,1,0:T(2,128)(2,1)S(1)} async-done(((bf16[32,2,3072]{2,1,0:T(2,128)(2,1)}), bf16[32,2,3072]{2,1,0:T(2,128)(2,1)S(1)}, u32[]{:S(2)}, u32[]{:S(2)}) %all-to-all-start.4) | async-done | bytes 393248 | tf_op jit(solution)/shard_map/all_to_all | solution.py:59
  450.4 26.3 %all-gather.13.cloned.1.call-done = bf16[768,2048]{1,0:T(8,128)(2,1)} async-done(((bf16[96,2048]{1,0:T(8,128)(2,1)}), bf16[768,2048]{1,0:T(8,128)(2,1)}) %all-gather.13.cloned.1.call-update) | async-done | bytes 3145744 | tf_op jit(solution)/shard_map/all_gather | solution.py:12
  476.7 2.5 reduce_sum.250
  479.2 1.0 all_to_all.61
  480.2 13.2 %all-to-all-start.7 = ((bf16[32,3,2048]{2,1,0:T(4,128)(2,1)}), bf16[32,3,2048]{2,1,0:T(4,128)(2,1)S(1)}, u32[]{:S(2)}, u32[]{:S(2)}) async-start(bf16[32,3,2048]{2,1,0:T(4,128)(2,1)} %all_to_all.61), calls=%async_computation.7 | async-start | bytes 1048576 | tf_op jit(solution)/shard_map/all_to_all | solution.py:65
  493.5 33.3 %all-to-all-done.7 = bf16[32,3,2048]{2,1,0:T(4,128)(2,1)S(1)} async-done(((bf16[32,3,2048]{2,1,0:T(4,128)(2,1)}), bf16[32,3,2048]{2,1,0:T(4,128)(2,1)S(1)}, u32[]{:S(2)}, u32[]{:S(2)}) %all-to-all-start.7) | async-done | bytes 393248 | tf_op jit(solution)/shard_map/all_to_all | solution.py:65
  527.9 0.8 reduce.9
  528.7 1.0 reshape.307
  529.7 3.9 all-to-all-start.8
  533.7 27.0 %all-to-all-done.8 = bf16[32,2,3072]{2,1,0:T(2,128)(2,1)S(1)} async-done(((bf16[32,2,3072]{2,1,0:T(2,128)(2,1)}), bf16[32,2,3072]{2,1,0:T(2,128)(2,1)S(1)}, u32[]{:S(2)}, u32[]{:S(2)}) %all-to-all-start.8) | async-done | bytes 393248 | tf_op jit(solution)/shard_map/all_to_all | solution.py:59
  561.8 26.3 %all-gather.15.cloned.1.call-done = bf16[768,2048]{1,0:T(8,128)(2,1)} async-done(((bf16[96,2048]{1,0:T(8,128)(2,1)}), bf16[768,2048]{1,0:T(8,128)(2,1)}) %all-gather.15.cloned.1.call-update) | async-done | bytes 3145744 | tf_op jit(solution)/shard_map/all_gather | solution.py:12
  588.1 2.5 reduce_sum.256
  590.8 46.4 %all_to_all.78 = bf16[32,3,2048]{2,1,0:T(4,128)(2,1)S(1)} all-to-all(bf16[32,3,2048]{2,1,0:T(4,128)(2,1)S(1)} %all_to_all.65), channel_id=1, replica_groups=mesh['sect'=2,'exp'=32,'dp'=8] {'exp'}, dimensions={0} | all-to-all | bytes 786432 | tf_op jit(solution)/shard_map/all_to_all | solution.py:65
  637.8 2.7 collective-permute-start.2
  640.6 4.9 collective-permute-done.2
  (141 shorter events, 19.1 us)
Async XLA Ops:
  16.1 45.0 %copy-start.14 = (bf16[1,1,192,2048]{3,2,1,0:T(8,128)(2,1)S(1)}, bf16[1,1,192,2048]{3,2,1,0:T(8,128)(2,1)}, u32[]{:S(2)}) copy-start(bf16[1,1,192,2048]{3,2,1,0:T(8,128)(2,1)} %param.28) | copy-start | bytes 2359300
  17.1 43.7 %all-to-all-start = ((bf16[32,2,3072]{2,1,0:T(2,128)(2,1)}), bf16[32,2,3072]{2,1,0:T(2,128)(2,1)S(1)}, u32[]{:S(2)}, u32[]{:S(2)}) async-start(bf16[32,2,3072]{2,1,0:T(2,128)(2,1)} %reshape.301), calls=%async_computation | async-start | bytes 786432 | tf_op jit(solution)/shard_map/all_to_all | solution.py:59
  33.3 56.2 %all-gather.9.cloned.1.call-start = ((), (), s32[]{:S(2)}) async-start(), calls=%async_computation.10 | async-start | bytes 3538944 | tf_op jit(solution)/shard_map/all_gather | solution.py:12
  61.1 0.9 copy-start.9
  61.1 1.1 copy-start.10
  61.2 0.7 copy-start.2
  61.2 6.3 copy-start.13
  61.2 6.7 %copy-start.16 = (s32[1,32]{1,0:T(1,128)S(1)}, s32[1,32]{1,0:T(1,128)}, u32[]{:S(2)}) copy-start(s32[1,32]{1,0:T(1,128)} %param.33) | copy-start | bytes 388
  63.1 43.6 %collective-permute-start = (bf16[32,2,2048]{2,1,0:T(2,128)(2,1)S(1)}, bf16[32,2,2048]{2,1,0:T(2,128)(2,1)S(1)}, u32[]{:S(2)}, u32[]{:S(2)}) collective-permute-start(bf16[32,2,2048]{2,1,0:T(2,128)(2,1)S(1)} %pad_maximum_fusion.2), channel_id=1, source_target_pairs={{0,256},{256,0},{1,257},{257,1},{2,258},{258,2},{3,259},{259,3},{4... | collective-permute-start | bytes 786440 | tf_op jit(solution)/shard_map/ppermute | solution.py:20
  93.1 46.6 %all-to-all-start.1 = ((bf16[32,3,2048]{2,1,0:T(4,128)(2,1)}), bf16[32,3,2048]{2,1,0:T(4,128)(2,1)S(1)}, u32[]{:S(2)}, u32[]{:S(2)}) async-start(bf16[32,3,2048]{2,1,0:T(4,128)(2,1)} %all_to_all.51), calls=%async_computation.1 | async-start | bytes 1048576 | tf_op jit(solution)/shard_map/all_to_all | solution.py:65
  112.7 31.1 %copy-start.11 = (s32[128,2]{0,1:T(2,128)S(1)}, s32[128,2]{0,1:T(2,128)}, u32[]{:S(2)}) copy-start(s32[128,2]{0,1:T(2,128)} %param.34) | copy-start | bytes 3076
  112.7 32.8 %copy-start.6 = (bf16[32,2048]{1,0:T(8,128)(2,1)S(1)}, bf16[32,2048]{1,0:T(8,128)(2,1)}, u32[]{:S(2)}) copy-start(bf16[32,2048]{1,0:T(8,128)(2,1)} %param.24) | copy-start | bytes 393220
  139.7 57.4 %all-to-all-start.5 = ((bf16[128,2,2048]{2,1,0:T(2,128)(2,1)}), bf16[128,2,2048]{2,1,0:T(2,128)(2,1)S(1)}, u32[]{:S(2)}, u32[]{:S(2)}) async-start(bf16[128,2,2048]{2,1,0:T(2,128)(2,1)} %broadcast_select_fusion.1), calls=%async_computation.5 | async-start | bytes 2097152 | tf_op jit(solution)/shard_map/all_to_all | solution.py:179
  143.8 2.1 copy-start.8
  197.1 32.2 %all-to-all-start.2 = ((bf16[32,2,3072]{2,1,0:T(2,128)(2,1)}), bf16[32,2,3072]{2,1,0:T(2,128)(2,1)S(1)}, u32[]{:S(2)}, u32[]{:S(2)}) async-start(bf16[32,2,3072]{2,1,0:T(2,128)(2,1)} %reshape.303), calls=%async_computation.2 | async-start | bytes 786432 | tf_op jit(solution)/shard_map/all_to_all | solution.py:59
  204.2 0.7 copy-start.12
  229.2 0.7 copy-start.5
  230.0 143.1 %all-to-all-start.6 = ((bf16[384,2,2048]{2,1,0:T(2,128)(2,1)}), bf16[384,2,2048]{2,1,0:T(2,128)(2,1)S(1)}, u32[]{:S(2)}, u32[]{:S(2)}) async-start(bf16[384,2,2048]{2,1,0:T(2,128)(2,1)} %copy.159), calls=%async_computation.6 | async-start | bytes 6291456 | tf_op jit(solution)/shard_map/all_to_all | solution.py:59
  234.1 40.7 %all-gather.11.cloned.1.call-start = ((), (), s32[]{:S(2)}) async-start(), calls=%async_computation.11 | async-start | bytes 3538944 | tf_op jit(solution)/shard_map/all_gather | solution.py:12
  373.1 41.6 %all-to-all-start.3 = ((bf16[32,3,2048]{2,1,0:T(4,128)(2,1)}), bf16[32,3,2048]{2,1,0:T(4,128)(2,1)}, u32[]{:S(2)}, u32[]{:S(2)}) async-start(bf16[32,3,2048]{2,1,0:T(4,128)(2,1)} %all_to_all.55), calls=%async_computation.3 | async-start | bytes 1048576 | tf_op jit(solution)/shard_map/all_to_all | solution.py:65
  381.8 1.4 copy-start.15
  383.1 1.7 copy-start
  384.9 4.8 copy-start.1
  389.6 1.9 copy-start.7
  391.7 44.9 %collective-permute-start.1 = (bf16[2,192,2048]{2,1,0:T(8,128)(2,1)S(1)}, bf16[2,192,2048]{2,1,0:T(8,128)(2,1)}, u32[]{:S(2)}, u32[]{:S(2)}) collective-permute-start(bf16[2,192,2048]{2,1,0:T(8,128)(2,1)S(1)} %get-tuple-element.162), channel_id=1, source_target_pairs={{0,256},{256,0},{1,257},{257,1},{2,258},{258,2},{3,259},{259,3},{4... | collective-permute-start | bytes 4718600 | tf_op jit(solution)/shard_map/ppermute | solution.py:20
  418.6 30.6 %all-to-all-start.4 = ((bf16[32,2,3072]{2,1,0:T(2,128)(2,1)}), bf16[32,2,3072]{2,1,0:T(2,128)(2,1)S(1)}, u32[]{:S(2)}, u32[]{:S(2)}) async-start(bf16[32,2,3072]{2,1,0:T(2,128)(2,1)} %reshape.305), calls=%async_computation.4 | async-start | bytes 786432 | tf_op jit(solution)/shard_map/all_to_all | solution.py:59
  422.5 54.2 %all-gather.13.cloned.1.call-start = ((), (), s32[]{:S(2)}) async-start(), calls=%async_computation.12 | async-start | bytes 3538944 | tf_op jit(solution)/shard_map/all_gather | solution.py:12
  449.7 0.7 copy-start.3
  480.2 46.6 %all-to-all-start.7 = ((bf16[32,3,2048]{2,1,0:T(4,128)(2,1)}), bf16[32,3,2048]{2,1,0:T(4,128)(2,1)S(1)}, u32[]{:S(2)}, u32[]{:S(2)}) async-start(bf16[32,3,2048]{2,1,0:T(4,128)(2,1)} %all_to_all.61), calls=%async_computation.7 | async-start | bytes 1048576 | tf_op jit(solution)/shard_map/all_to_all | solution.py:65
  529.7 30.9 %all-to-all-start.8 = ((bf16[32,2,3072]{2,1,0:T(2,128)(2,1)}), bf16[32,2,3072]{2,1,0:T(2,128)(2,1)S(1)}, u32[]{:S(2)}, u32[]{:S(2)}) async-start(bf16[32,2,3072]{2,1,0:T(2,128)(2,1)} %reshape.307), calls=%async_computation.8 | async-start | bytes 786432 | tf_op jit(solution)/shard_map/all_to_all | solution.py:59
  533.6 54.5 %all-gather.15.cloned.1.call-start = ((), (), s32[]{:S(2)}) async-start(), calls=%async_computation.13 | async-start | bytes 3538944 | tf_op jit(solution)/shard_map/all_gather | solution.py:12
  561.0 0.7 copy-start.4
  637.8 7.7 %collective-permute-start.2 = (bf16[32,1024]{1,0:T(8,128)(2,1)S(1)}, bf16[32,1024]{1,0:T(8,128)(2,1)S(1)}, u32[]{:S(2)}, u32[]{:S(2)}) collective-permute-start(bf16[32,1024]{1,0:T(8,128)(2,1)S(1)} %slice.87), channel_id=1, source_target_pairs={{0,256},{256,0},{1,257},{257,1},{2,258},{258,2},{3,259},{259,3},{4... | collective-permute-start | bytes 196616 | tf_op jit(solution)/shard_map/ppermute | solution.py:20
Sparse Core Ops, SparseCore 0:
  62.1 27.3 all-gather.8
  238.5 36.1 all-gather.10
  450.6 26.1 all-gather.12
  561.9 26.1 all-gather.14
